TPU v7x, 512 devices: a whole 4x4x16 slice. The times are simulated.
512 devices in a mesh: view: 4 (over x), dev: 128 (over z, y, core).
Axes of the slice: x: 4, y: 4, z: 16, core: 2. Of those that a mesh axis runs over, the one named last changes fastest.
Arguments:
- attributes: float32 [59, 65536], P(None, 'dev'), may hold values from -6 to 8, as said below
- camera: float32 [4, 6], P('view'), may hold values from -0.2 to 0.2
- list_owner: int32 [4, 512, 256, 1], P('view', 'dev'), may hold values from 0 to 127; in each aligned block of 1024 rows (0 to 1023, 1024 to 2047, ..., all dimensions but the last counted through in order) at most 16 rows name the same one
- list_local: int32 [4, 512, 256], P('view', 'dev'), may hold values from 0 to 511
- term_depth: int32 [4, 512, 256], P('view', 'dev'), may hold values from 1 to 256
- image_cot: float32 [4, 3, 512, 256], P('view', None, 'dev'), may hold values from -6 to 6
Outputs:
- image: float32 [4, 3, 512, 256], P('view', None, 'dev')
- attr_grad: float32 [59, 65536], P(None, 'dev')
Inputs may be any that keep to these rules, and one draw needn't show every extreme that they name: `attributes`: the quaternion's real part lies in 0.5 to 1.5, the third position coordinate in 4 to 8. `list_owner`: among the slots of one device's tiles of one view no owner is named more than 16 times.
All inputs are finite; a program needn't handle non-finite values.
Results may differ from a plain program's by a relative error of at most 0.0003.
Values sent between devices are 32-bit elements; how exact they have to be, the bound alone decides.
No kernel may reach another device: no remote copies, remote signals or barrier semaphores. Data moves between devices by JAX's collectives and lax.ppermute only.
A program may use at most 64 MiB of HBM per device.

v0:
```python
import jax
import jax.numpy as jnp
from jax import lax
from jax.sharding import PartitionSpec as P

TILE_COLS = 16
SH_C0 = 0.28209479177387814
SH_C1 = 0.4886025119029199
SH_C2 = (
    1.0925484305920792,
    -1.0925484305920792,
    0.31539156525252005,
    -1.0925484305920792,
    0.5462742152960396,
)
SH_C3 = (
    -0.5900435899266435,
    2.890611442640554,
    -0.4570457994644658,
    0.3731763325901154,
    -0.4570457994644658,
    1.445305721320277,
    -0.5900435899266435,
)
BLUR = 1e-05


def rotation(angles):
    one = jnp.ones((), jnp.float32)
    zero = jnp.zeros((), jnp.float32)
    cosx, sinx = (jnp.cos(angles[0]), jnp.sin(angles[0]))
    cosy, siny = (jnp.cos(angles[1]), jnp.sin(angles[1]))
    cosz, sinz = (jnp.cos(angles[2]), jnp.sin(angles[2]))
    rot_x = jnp.stack(
        [
            jnp.stack([one, zero, zero]),
            jnp.stack([zero, cosx, -sinx]),
            jnp.stack([zero, sinx, cosx]),
        ]
    )
    rot_y = jnp.stack(
        [
            jnp.stack([cosy, zero, siny]),
            jnp.stack([zero, one, zero]),
            jnp.stack([-siny, zero, cosy]),
        ]
    )
    rot_z = jnp.stack(
        [
            jnp.stack([cosz, -sinz, zero]),
            jnp.stack([sinz, cosz, zero]),
            jnp.stack([zero, zero, one]),
        ]
    )
    high = lax.Precision.HIGHEST
    return jnp.dot(rot_z, jnp.dot(rot_y, rot_x, precision=high), precision=high)


def harmonics(dirx, diry, dirz):
    xx, yy, zz = (dirx * dirx, diry * diry, dirz * dirz)
    return [
        SH_C0 + 0.0 * dirx,
        -SH_C1 * diry,
        SH_C1 * dirz,
        -SH_C1 * dirx,
        SH_C2[0] * dirx * diry,
        SH_C2[1] * diry * dirz,
        SH_C2[2] * (2.0 * zz - xx - yy),
        SH_C2[3] * dirx * dirz,
        SH_C2[4] * (xx - yy),
        SH_C3[0] * diry * (3.0 * xx - yy),
        SH_C3[1] * dirx * diry * dirz,
        SH_C3[2] * diry * (4.0 * zz - xx - yy),
        SH_C3[3] * dirz * (2.0 * zz - 3.0 * xx - 3.0 * yy),
        SH_C3[4] * dirx * (4.0 * zz - xx - yy),
        SH_C3[5] * dirz * (xx - yy),
        SH_C3[6] * dirx * (xx - 3.0 * yy),
    ]


def project(attrs, cam):
    rot = rotation(cam[0:3])
    shift = cam[3:6]
    pos = attrs[0:3]
    campos = jnp.dot(rot, pos, precision=lax.Precision.HIGHEST) + shift[:, None]
    posx, posy, posz = (campos[0], campos[1], campos[2])
    inverse = 1.0 / posz
    jac = [
        [inverse, 0.0 * inverse, -posx * inverse * inverse],
        [0.0 * inverse, inverse, -posy * inverse * inverse],
    ]
    tmat = [[sum((jac[r][i] * rot[i, j] for i in range(3))) for j in range(3)] for r in range(2)]
    scale = jnp.exp(attrs[3:6])
    quat = attrs[6:10]
    quat = quat * lax.rsqrt(jnp.sum(quat * quat, axis=0))
    qw, qa, qb, qc = (quat[0], quat[1], quat[2], quat[3])
    rgau = [
        [1 - 2 * (qb * qb + qc * qc), 2 * (qa * qb - qw * qc), 2 * (qa * qc + qw * qb)],
        [2 * (qa * qb + qw * qc), 1 - 2 * (qa * qa + qc * qc), 2 * (qb * qc - qw * qa)],
        [2 * (qa * qc - qw * qb), 2 * (qb * qc + qw * qa), 1 - 2 * (qa * qa + qb * qb)],
    ]
    mscaled = [[rgau[i][k] * scale[k] for k in range(3)] for i in range(3)]
    cov = [
        [sum((mscaled[i][k] * mscaled[j][k] for k in range(3))) for j in range(3)] for i in range(3)
    ]
    sig = [
        [
            sum((tmat[r][i] * cov[i][j] * tmat[s][j] for i in range(3) for j in range(3)))
            for s in range(2)
        ]
        for r in range(2)
    ]
    sig_a = sig[0][0] + BLUR
    sig_b = sig[0][1]
    sig_c = sig[1][1] + BLUR
    det = sig_a * sig_c - sig_b * sig_b
    centre = [
        -(rot[0, j] * shift[0] + rot[1, j] * shift[1] + rot[2, j] * shift[2]) for j in range(3)
    ]
    dirs = [pos[j] - centre[j] for j in range(3)]
    norm_inv = lax.rsqrt(dirs[0] * dirs[0] + dirs[1] * dirs[1] + dirs[2] * dirs[2])
    basis = harmonics(dirs[0] * norm_inv, dirs[1] * norm_inv, dirs[2] * norm_inv)
    colors = [0.5 + sum((basis[k] * attrs[11 + 3 * k + ch] for k in range(16))) for ch in range(3)]
    opacity = jax.nn.sigmoid(attrs[10])
    return jnp.stack(
        [posx * inverse, posy * inverse, sig_c / det, -sig_b / det, sig_a / det, opacity] + colors
    )


def pixel_coords(tile, ntiles):
    pixel = jnp.arange(256, dtype=jnp.int32)
    col = tile % TILE_COLS
    row = tile // TILE_COLS
    xs = ((col * 16 + pixel % 16).astype(jnp.float32) + 0.5) / (16.0 * TILE_COLS) - 0.5
    ys = ((row * 16 + pixel // 16).astype(jnp.float32) + 0.5) / (16.0 * (ntiles // TILE_COLS)) - 0.5
    return (xs, ys)


def tile_color(rows, xs, ys, depth):
    slot_entries = rows.shape[1]
    delta_x = xs[:, None] - rows[0][None, :]
    delta_y = ys[:, None] - rows[1][None, :]
    power = (
        0.5 * (rows[2][None, :] * delta_x * delta_x + rows[4][None, :] * delta_y * delta_y)
        + rows[3][None, :] * delta_x * delta_y
    )
    live = (jnp.arange(slot_entries, dtype=jnp.int32)[None, :] < depth[:, None]).astype(jnp.float32)
    alpha = rows[5][None, :] * jnp.exp(-power) * live
    keep = jnp.cumprod(1.0 - alpha, axis=1)
    trans = jnp.concatenate([jnp.ones((xs.shape[0], 1), jnp.float32), keep[:, :-1]], axis=1)
    weight = trans * alpha
    return jnp.einsum("ps,cs->cp", weight, rows[6:9], precision=lax.Precision.HIGHEST)


def composite(rows_slot, first_tile, ntiles, depth, cotangent):
    tile_entries = depth.shape[0]
    rows_tiles = jnp.transpose(rows_slot.reshape(rows_slot.shape[0], tile_entries, -1), (1, 0, 2))

    def tile_work(packed):
        rows, tile, pixel_depth, pixel_cot = packed
        xs, ys = pixel_coords(tile, ntiles)
        color, pull = jax.vjp(lambda r: tile_color(r, xs, ys, pixel_depth), rows)
        return (color, pull(pixel_cot)[0])

    tile_ids = first_tile + jnp.arange(tile_entries, dtype=jnp.int32)
    color, grads = lax.map(tile_work, (rows_tiles, tile_ids, depth, cotangent))
    return (color, jnp.transpose(grads, (1, 0, 2)).reshape(rows_slot.shape[0], -1))


def per_device(attributes, camera, list_owner, list_local, term_depth, image_cot):
    device_total = lax.axis_size("dev")
    g_dev = attributes.shape[1]
    tile_entries = list_local.shape[1]
    slot_entries = list_local.shape[2]
    slot_total = tile_entries * slot_entries
    slot_capacity = 2 * slot_total // device_total
    ntiles = tile_entries * device_total
    owner = list_owner[0, :, :, 0].reshape(-1)
    local_ids = list_local[0].reshape(-1)
    onehot = (owner[:, None] == jnp.arange(device_total, dtype=jnp.int32)[None, :]).astype(
        jnp.int32
    )
    counts = jnp.sum(onehot, axis=0)
    starts = jnp.cumsum(counts) - counts
    initial_slot = jnp.sum(onehot * starts[None, :], axis=1)
    sorted_order = jnp.argsort(owner, stable=True)
    rank = (
        jnp.zeros((slot_total,), jnp.int32)
        .at[sorted_order]
        .set(jnp.arange(slot_total, dtype=jnp.int32) - initial_slot[sorted_order])
    )
    position = owner * slot_capacity + rank
    request = jnp.zeros((device_total * slot_capacity,), jnp.int32).at[position].set(local_ids)
    asked = lax.all_to_all(
        request.reshape(device_total, slot_capacity), "dev", split_axis=0, concat_axis=0, tiled=True
    ).reshape(-1)
    cam = camera[0]
    first_tile = lax.axis_index("dev") * tile_entries
    depth = term_depth[0]
    cotangent = jnp.transpose(image_cot[0], (1, 0, 2))
    total = None
    rows_owner, pull_owner = jax.vjp(lambda a: project(a, cam), attributes)
    sent = rows_owner[:, asked]
    arrived = lax.all_to_all(
        sent.reshape(9, device_total, slot_capacity), "dev", split_axis=1, concat_axis=1, tiled=True
    ).reshape(9, -1)
    rows_slot = arrived[:, position]
    color, grad_slot = composite(rows_slot, first_tile, ntiles, depth, cotangent)
    grad_buffer = (
        jnp.zeros((9, device_total * slot_capacity), jnp.float32).at[:, position].set(grad_slot)
    )
    returned = lax.all_to_all(
        grad_buffer.reshape(9, device_total, slot_capacity),
        "dev",
        split_axis=1,
        concat_axis=1,
        tiled=True,
    ).reshape(9, -1)
    grad_rows = jnp.zeros((9, g_dev), jnp.float32).at[:, asked].add(returned)
    attr_grad = pull_owner(grad_rows)[0]
    total = lax.psum(attr_grad, "view")
    image = jnp.transpose(color, (1, 0, 2))[None]
    return (image, total)


def solution(mesh):
    in_specs = (
        P(None, "dev"),
        P("view", None),
        P("view", "dev", None, None),
        P("view", "dev", None),
        P("view", "dev", None),
        P("view", None, "dev", None),
    )
    out_specs = (P("view", None, "dev", None), P(None, "dev"))
    return jax.shard_map(
        per_device, mesh=mesh, in_specs=in_specs, out_specs=out_specs, check_vma=False
    )
```

profile of v0, /device:TPU:8, one launch (start us, length us, event | category | flops | bytes accessed | tf_op | source)
XLA Modules:
  0.0 316.3 jit_solution(12072224999658758813)
XLA Ops:
  7.2 0.9 convert_reduce_fusion
  8.8 4.4 %sort.17 = (s32[1024]{0:T(1024)}, s32[1024]{0:T(1024)S(1)}) sort(s32[1024]{0:T(1024)S(1)} %bitcast.195, s32[1024]{0:T(1024)S(1)} %iota.41), dimensions={0}, to_apply=%region_1.0 | sort | flops 10240 | bytes 16384 | tf_op jit(solution)/shard_map/jit(argsort)/sort | solution.py:186
  13.9 4.5 %gather_fusion = s32[1024]{0:T(1024)S(1)} fusion(s32[1024]{0:T(1024)S(1)} %select_reduce_fusion, s32[1024]{0:T(1024)S(1)} %get-tuple-element.358), kind=kCustom, calls=%fused_computation | custom fusion | bytes 12288 | tf_op jit(solution)/shard_map/gather | solution.py:190
  18.5 4.3 %scatter_custom_fusion = s32[1024]{0:T(1024)S(1)} fusion(s32[1024]{0:T(1024)S(1)} %get-tuple-element.359, s32[1024]{0:T(1024)S(1)} %iota_subtract_fusion, s32[]{:T(128)} %constant.192.clone.1), kind=kCustom, calls=%fused_computation.292 | custom fusion | bytes 4100 | tf_op jit(solution)/shard_map/scatter | solution.py:190
  22.8 4.3 %scatter_custom_fusion.1 = s32[2048]{0:T(1024)S(1)} fusion(s32[1024]{0:T(1024)S(1)} %get-tuple-element.215, s32[1024]{0:T(1024)S(1)} %bitcast.202, s32[]{:T(128)} %constant.192.clone.1), kind=kCustom, calls=%fused_computation.165 | custom fusion | bytes 8196 | tf_op jit(solution)/shard_map/scatter | solution.py:193
  27.9 19.5 %all-to-all-start = ((s32[128,1,16]{2,1,0:T(1,128)}), s32[128,1,16]{2,1,0:T(1,128)S(1)}, u32[]{:S(2)}, u32[]{:S(2)}) async-start(s32[128,1,16]{2,1,0:T(1,128)} %bitcast.48), calls=%async_computation | async-start | bytes 131072 | tf_op jit(solution)/shard_map/all_to_all | solution.py:194
  74.5 2.1 fusion.143
  77.4 0.8 reduce.4
  78.4 5.5 %gather_fusion.1 = f32[2048,9]{1,0:T(8,128)S(1)} fusion(f32[9,512]{0,1:T(8,128)S(1)} %copy.57, s32[2048]{0:T(1024)S(1)} %broadcast_clamp_fusion), kind=kCustom, calls=%fused_computation.1 | custom fusion | bytes 155648 | tf_op jit(solution)/shard_map/gather | solution.py:203
  83.8 1.4 reshape.321
  85.3 16.2 %all-to-all-start.1 = ((f32[128,1,144]{2,1,0:T(1,128)}), f32[128,1,144]{2,1,0:T(1,128)S(1)}, u32[]{:S(2)}, u32[]{:S(2)}) async-start(f32[128,1,144]{2,1,0:T(1,128)} %reshape.321), calls=%async_computation.1 | async-start | bytes 262144 | tf_op jit(solution)/shard_map/all_to_all | solution.py:204
  101.8 15.8 %all-to-all-done.1 = f32[128,1,144]{2,1,0:T(1,128)S(1)} async-done(((f32[128,1,144]{2,1,0:T(1,128)}), f32[128,1,144]{2,1,0:T(1,128)S(1)}, u32[]{:S(2)}, u32[]{:S(2)}) %all-to-all-start.1) | async-done | bytes 73760 | tf_op jit(solution)/shard_map/all_to_all | solution.py:204
  118.2 0.9 reduce.5
  119.8 2.8 gather_fusion.2
  123.4 82.5 %while.15 = (s32[]{:T(128)}, f32[4,3,256]{2,0,1:T(4,128)S(1)}, f32[4,9,256]{2,1,0:T(8,128)S(1)}, f32[4,9,256]{2,1,0:T(8,128)S(1)}, s32[4,256]{1,0:T(4,128)}, /*i...) while((s32[]{:T(128)}, f32[4,3,256]{2,0,1:T(4,128)S(1)}, ...), condition=%wide.region_14.15_spmd, body=%wide.region_7.14_spmd.sunk | while | flops 15078685 | bytes 22935272 | solution.py:166
  206.8 3.3 %scatter_custom_fusion.2 = f32[9,2048]{0,1:T(8,128)S(1)} fusion(s32[1024]{0:T(1024)S(1)} %get-tuple-element.215, f32[1024,9]{1,0:T(8,128)S(1)} %copy.62, f32[]{:T(128)} %constant.193.clone.1), kind=kCustom, calls=%fused_computation.138 | custom fusion | bytes 73732 | tf_op jit(solution)/shard_map/scatter | solution.py:210
  210.9 23.2 %all_to_all.19 = f32[128,1,144]{2,1,0:T(1,128)S(1)} all-to-all(f32[128,1,144]{2,1,0:T(1,128)S(1)} %reshape.323), channel_id=1, replica_groups=mesh['view'=4,'dev'=128] {'dev'}, dimensions={0} | all-to-all | bytes 147456 | tf_op jit(solution)/shard_map/all_to_all | solution.py:212
  234.0 0.9 reduce.6
  235.6 12.1 %scatter_custom_fusion.3 = f32[9,512]{0,1:T(8,128)S(1)} fusion(s32[2048]{0:T(1024)S(1)} %bitcast.199, f32[2048,9]{1,0:T(8,128)S(1)} %bitcast.148, f32[]{:T(128)} %constant.193.clone.1), kind=kCustom, calls=%fused_computation.144 | custom fusion | flops 18432 | bytes 18436 | tf_op jit(solution)/shard_map/scatter-add | solution.py:219
  250.3 5.8 %fusion.98 = (f32[1,512]{1,0:T(1,128)S(1)}, f32[1,512]{1,0:T(1,128)S(1)}, f32[1,512]{1,0:T(1,128)S(1)}, f32[1,512]{1,0:T(1,128)S(1)}, f32[1,512]{1,0:T(1,128)S(1...) fusion(f32[1,512]{1,0:T(1,128)S(1)} %copy.82, f32[1,512]{1,0:T(1,128)S(1)} %copy.81, ...), kind=kLoop, calls=%fused_computation.325 | loop fusion | flops 81920 | bytes 100388 | tf_op jit(solution)/shard_map/transpose(jvp())/neg | solution.py:87
  256.1 2.0 negate_add_fusion.1
  258.4 0.9 pad_add_fusion.9
  259.3 48.5 %all-reduce.135.cloned.1.call-done = f32[59,512]{1,0:T(8,128)} async-done(((f32[59,512]{1,0:T(8,128)}), f32[59,512]{1,0:T(8,128)}) %all-reduce.135.cloned.1.call-update) | async-done | bytes 120848 | tf_op jit(solution)/shard_map/psum | solution.py:221
  307.8 1.6 copy.180
  (881 shorter events, 82.9 us)
Async XLA Ops:
  18.5 28.9 %copy-start.11 = (f32[59,512]{1,0:T(8,128)S(1)}, f32[59,512]{1,0:T(8,128)}, u32[]{:S(2)}) copy-start(f32[59,512]{1,0:T(8,128)} %param.8) | copy-start | bytes 362500
  27.9 49.1 %all-to-all-start = ((s32[128,1,16]{2,1,0:T(1,128)}), s32[128,1,16]{2,1,0:T(1,128)S(1)}, u32[]{:S(2)}, u32[]{:S(2)}) async-start(s32[128,1,16]{2,1,0:T(1,128)} %bitcast.48), calls=%async_computation | async-start | bytes 131072 | tf_op jit(solution)/shard_map/all_to_all | solution.py:194
  85.3 16.5 %copy-start.15 = (f32[1,3,4,256]{3,2,1,0:T(4,128)S(1)}, f32[1,3,4,256]{3,2,1,0:T(4,128)}, u32[]{:S(2)}) copy-start(f32[1,3,4,256]{3,2,1,0:T(4,128)} %param.13) | copy-start | bytes 36868
  85.3 32.3 %all-to-all-start.1 = ((f32[128,1,144]{2,1,0:T(1,128)}), f32[128,1,144]{2,1,0:T(1,128)S(1)}, u32[]{:S(2)}, u32[]{:S(2)}) async-start(f32[128,1,144]{2,1,0:T(1,128)} %reshape.321), calls=%async_computation.1 | async-start | bytes 262144 | tf_op jit(solution)/shard_map/all_to_all | solution.py:204
  101.5 206.3 %all-reduce.135.cloned.1.call-start = ((), (), s32[]{:S(2)}) async-start(), calls=%async_computation.3 | async-start | bytes 262144 | tf_op jit(solution)/shard_map/psum | solution.py:221
  128.3 11.2 %copy-start = (f32[256,128]{0,1:T(8,128)}, f32[256,128]{0,1:T(8,128)S(1)}, u32[]{:S(2)}) copy-start(f32[256,128]{0,1:T(8,128)S(1)} %slice.1658) | copy-start | bytes 393220 | tf_op jit(solution)/shard_map/while
  132.4 5.5 %copy-start.2 = (f32[256,64]{0,1:T(8,128)}, f32[256,64]{0,1:T(8,128)S(1)}, u32[]{:S(2)}) copy-start(f32[256,64]{0,1:T(8,128)S(1)} %slice.1665) | copy-start | bytes 196612 | tf_op jit(solution)/shard_map/while
  132.5 4.0 %copy-start.4 = (f32[256,32]{0,1:T(8,128)}, f32[256,32]{0,1:T(8,128)S(1)}, u32[]{:S(2)}) copy-start(f32[256,32]{0,1:T(8,128)S(1)} %slice.1666) | copy-start | bytes 98308 | tf_op jit(solution)/shard_map/while
  132.6 2.4 copy-start.6
  132.7 1.6 copy-start.8
  148.9 11.2 %copy-start = (f32[256,128]{0,1:T(8,128)}, f32[256,128]{0,1:T(8,128)S(1)}, u32[]{:S(2)}) copy-start(f32[256,128]{0,1:T(8,128)S(1)} %slice.1658) | copy-start | bytes 393220 | tf_op jit(solution)/shard_map/while
  153.0 5.5 %copy-start.2 = (f32[256,64]{0,1:T(8,128)}, f32[256,64]{0,1:T(8,128)S(1)}, u32[]{:S(2)}) copy-start(f32[256,64]{0,1:T(8,128)S(1)} %slice.1665) | copy-start | bytes 196612 | tf_op jit(solution)/shard_map/while
  153.1 4.0 %copy-start.4 = (f32[256,32]{0,1:T(8,128)}, f32[256,32]{0,1:T(8,128)S(1)}, u32[]{:S(2)}) copy-start(f32[256,32]{0,1:T(8,128)S(1)} %slice.1666) | copy-start | bytes 98308 | tf_op jit(solution)/shard_map/while
  153.2 2.4 copy-start.6
  153.3 1.6 copy-start.8
  169.5 11.2 %copy-start = (f32[256,128]{0,1:T(8,128)}, f32[256,128]{0,1:T(8,128)S(1)}, u32[]{:S(2)}) copy-start(f32[256,128]{0,1:T(8,128)S(1)} %slice.1658) | copy-start | bytes 393220 | tf_op jit(solution)/shard_map/while
  173.6 5.5 %copy-start.2 = (f32[256,64]{0,1:T(8,128)}, f32[256,64]{0,1:T(8,128)S(1)}, u32[]{:S(2)}) copy-start(f32[256,64]{0,1:T(8,128)S(1)} %slice.1665) | copy-start | bytes 196612 | tf_op jit(solution)/shard_map/while
  173.7 4.0 %copy-start.4 = (f32[256,32]{0,1:T(8,128)}, f32[256,32]{0,1:T(8,128)S(1)}, u32[]{:S(2)}) copy-start(f32[256,32]{0,1:T(8,128)S(1)} %slice.1666) | copy-start | bytes 98308 | tf_op jit(solution)/shard_map/while
  173.8 2.4 copy-start.6
  173.9 1.6 copy-start.8
  190.1 11.2 %copy-start = (f32[256,128]{0,1:T(8,128)}, f32[256,128]{0,1:T(8,128)S(1)}, u32[]{:S(2)}) copy-start(f32[256,128]{0,1:T(8,128)S(1)} %slice.1658) | copy-start | bytes 393220 | tf_op jit(solution)/shard_map/while
  194.3 5.5 %copy-start.2 = (f32[256,64]{0,1:T(8,128)}, f32[256,64]{0,1:T(8,128)S(1)}, u32[]{:S(2)}) copy-start(f32[256,64]{0,1:T(8,128)S(1)} %slice.1665) | copy-start | bytes 196612 | tf_op jit(solution)/shard_map/while
  194.4 4.0 %copy-start.4 = (f32[256,32]{0,1:T(8,128)}, f32[256,32]{0,1:T(8,128)S(1)}, u32[]{:S(2)}) copy-start(f32[256,32]{0,1:T(8,128)S(1)} %slice.1666) | copy-start | bytes 98308 | tf_op jit(solution)/shard_map/while
  194.5 2.4 copy-start.6
  (77 other events, 51.3 us)
Sparse Core Ops, SparseCore 0:
  259.4 48.3 all-reduce.134
where the time goes:
time: 318 us; the launch traced here: 316 us
  local copies, waits for them, and re-layouts  94.4 us (30%)
  waiting for transfers between devices  64.3 us (20%)
  other arithmetic  40.8 us (13%)
  between operations  37.4 us (12%)
  starting transfers between devices  36 us (11%)
  blocking collectives  23.2 us (7%)
  loops' own time  14 us (4%)
  matrix products  6.13 us (2%)
    psum x1, waiting for transfers between devices, per_device(): total = lax.psum(attr_grad, 'view')  48.5 us
    all_to_all x1, blocking collectives, per_device(): lax.all_to_all(grad_buffer.reshape(9, device_total, slot_capacity), 'dev'...  23.2 us
    all_to_all x1, starting transfers between devices, per_device(): lax.all_to_all(request.reshape(device_total, slot_capacity), 'dev', split...  19.5 us
    slice x180, local copies, waits for them, and re-layouts, tile_color(): keep = jnp.cumprod(1.0 - alpha, axis=1)  18.3 us
    all_to_all x1, starting transfers between devices, per_device(): lax.all_to_all(sent.reshape(9, device_total, slot_capacity), 'dev', split...  16.2 us
    all_to_all x1, waiting for transfers between devices, per_device(): lax.all_to_all(sent.reshape(9, device_total, slot_capacity), 'dev', split...  15.8 us
    split x48, local copies, waits for them, and re-layouts, tile_color(): keep = jnp.cumprod(1.0 - alpha, axis=1)  15.2 us
    another operation x1, loops' own time, composite(): color, grads = lax.map(tile_work, (rows_tiles, tile_ids, depth, cotangent))  14 us
  transfers between devices with their start and end apart: 3, of which 2 were waited for; matrix products, arithmetic and copies ran while one was open for 1% of the time, Pallas kernels for 0%

commit v1 on v0

--- a/solution.py
+++ b/solution.py
@@ -218,7 +218,9 @@
     ).reshape(9, -1)
     grad_rows = jnp.zeros((9, g_dev), jnp.float32).at[:, asked].add(returned)
     attr_grad = pull_owner(grad_rows)[0]
-    total = lax.psum(attr_grad, "view")
+    total = attr_grad
+    for hop in (1, 2):
+        total = total + lax.ppermute(total, "view", [(dev, dev ^ hop) for dev in range(4)])
     image = jnp.transpose(color, (1, 0, 2))[None]
     return (image, total)
 

time: 318 us -> 271 us (0.85)
  the two profiles are of different devices: /device:TPU:8 before, /device:TPU:38 now
where the time goes in v1:
time: 271 us; the launch traced here: 269 us
  local copies, waits for them, and re-layouts  92.7 us (34%)
  starting transfers between devices  41.4 us (15%)
  other arithmetic  39.7 us (15%)
  waiting for transfers between devices  27.7 us (10%)
  between operations  24 us (9%)
  blocking collectives  23.1 us (9%)
  loops' own time  14 us (5%)
  matrix products  6.13 us (2%)
    all_to_all x1, blocking collectives, per_device(): lax.all_to_all(grad_buffer.reshape(9, device_total, slot_capacity), 'dev'...  23.1 us
    all_to_all x1, starting transfers between devices, per_device(): lax.all_to_all(request.reshape(device_total, slot_capacity), 'dev', split...  19.2 us
    slice x180, local copies, waits for them, and re-layouts, tile_color(): keep = jnp.cumprod(1.0 - alpha, axis=1)  18.1 us
    all_to_all x1, waiting for transfers between devices, per_device(): lax.all_to_all(sent.reshape(9, device_total, slot_capacity), 'dev', split...  17.1 us
    all_to_all x1, starting transfers between devices, per_device(): lax.all_to_all(sent.reshape(9, device_total, slot_capacity), 'dev', split...  16.2 us
    split x48, local copies, waits for them, and re-layouts, tile_color(): keep = jnp.cumprod(1.0 - alpha, axis=1)  15.3 us
    another operation x1, loops' own time, composite(): color, grads = lax.map(tile_work, (rows_tiles, tile_ids, depth, cotangent))  14 us
    while x92, local copies, waits for them, and re-layouts  13.5 us
  transfers between devices with their start and end apart: 4, of which 3 were waited for; matrix products, arithmetic and copies ran while one was open for 2% of the time, Pallas kernels for 0%

profile of v1, /device:TPU:38, one launch (start us, length us, event | category | flops | bytes accessed | tf_op | source)
XLA Modules:
  0.0 268.8 jit_solution(13756329862446485010)
XLA Ops:
  0.6 0.9 convert_reduce_fusion
  2.3 4.4 %sort.17 = (s32[1024]{0:T(1024)}, s32[1024]{0:T(1024)S(1)}) sort(s32[1024]{0:T(1024)S(1)} %bitcast.195, s32[1024]{0:T(1024)S(1)} %iota.41), dimensions={0}, to_apply=%region_1.0 | sort | flops 10240 | bytes 16384 | tf_op jit(solution)/shard_map/jit(argsort)/sort | solution.py:186
  7.4 4.5 %gather_fusion = s32[1024]{0:T(1024)S(1)} fusion(s32[1024]{0:T(1024)S(1)} %select_reduce_fusion, s32[1024]{0:T(1024)S(1)} %get-tuple-element.358), kind=kCustom, calls=%fused_computation | custom fusion | bytes 12288 | tf_op jit(solution)/shard_map/gather | solution.py:190
  12.0 4.3 %scatter_custom_fusion = s32[1024]{0:T(1024)S(1)} fusion(s32[1024]{0:T(1024)S(1)} %get-tuple-element.359, s32[1024]{0:T(1024)S(1)} %iota_subtract_fusion, s32[]{:T(128)} %constant.192.clone.1), kind=kCustom, calls=%fused_computation.292 | custom fusion | bytes 4100 | tf_op jit(solution)/shard_map/scatter | solution.py:190
  16.3 4.3 %scatter_custom_fusion.1 = s32[2048]{0:T(1024)S(1)} fusion(s32[1024]{0:T(1024)S(1)} %get-tuple-element.215, s32[1024]{0:T(1024)S(1)} %bitcast.202, s32[]{:T(128)} %constant.192.clone.1), kind=kCustom, calls=%fused_computation.165 | custom fusion | bytes 8196 | tf_op jit(solution)/shard_map/scatter | solution.py:193
  21.3 19.2 %all-to-all-start = ((s32[128,1,16]{2,1,0:T(1,128)}), s32[128,1,16]{2,1,0:T(1,128)S(1)}, u32[]{:S(2)}, u32[]{:S(2)}) async-start(s32[128,1,16]{2,1,0:T(1,128)} %bitcast.48), calls=%async_computation | async-start | bytes 131072 | tf_op jit(solution)/shard_map/all_to_all | solution.py:194
  67.6 2.0 fusion.143
  71.3 5.5 %gather_fusion.1 = f32[2048,9]{1,0:T(8,128)S(1)} fusion(f32[9,512]{0,1:T(8,128)S(1)} %copy.57, s32[2048]{0:T(1024)S(1)} %broadcast_clamp_fusion), kind=kCustom, calls=%fused_computation.1 | custom fusion | bytes 155648 | tf_op jit(solution)/shard_map/gather | solution.py:203
  76.8 1.4 reshape.321
  78.2 16.2 %all-to-all-start.1 = ((f32[128,1,144]{2,1,0:T(1,128)}), f32[128,1,144]{2,1,0:T(1,128)S(1)}, u32[]{:S(2)}, u32[]{:S(2)}) async-start(f32[128,1,144]{2,1,0:T(1,128)} %reshape.321), calls=%async_computation.1 | async-start | bytes 262144 | tf_op jit(solution)/shard_map/all_to_all | solution.py:204
  94.5 17.1 %all-to-all-done.1 = f32[128,1,144]{2,1,0:T(1,128)S(1)} async-done(((f32[128,1,144]{2,1,0:T(1,128)}), f32[128,1,144]{2,1,0:T(1,128)S(1)}, u32[]{:S(2)}, u32[]{:S(2)}) %all-to-all-start.1) | async-done | bytes 73760 | tf_op jit(solution)/shard_map/all_to_all | solution.py:204
  112.1 0.9 reduce.5
  113.7 2.8 %gather_fusion.2 = f32[1024,9]{1,0:T(8,128)S(1)} fusion(f32[9,2048]{0,1:T(8,128)S(1)} %bitcast.146, s32[1024]{0:T(1024)S(1)} %get-tuple-element.214), kind=kCustom, calls=%fused_computation.2 | custom fusion | bytes 77824 | tf_op jit(solution)/shard_map/gather | solution.py:207
  117.3 82.3 %while.15 = (s32[]{:T(128)}, f32[4,3,256]{2,0,1:T(4,128)S(1)}, f32[4,9,256]{2,1,0:T(8,128)S(1)}, f32[4,9,256]{2,1,0:T(8,128)S(1)}, s32[4,256]{1,0:T(4,128)}, /*i...) while((s32[]{:T(128)}, f32[4,3,256]{2,0,1:T(4,128)S(1)}, ...), condition=%wide.region_14.15_spmd, body=%wide.region_7.14_spmd.sunk | while | flops 15078685 | bytes 22935272 | solution.py:166
  200.6 3.3 %scatter_custom_fusion.2 = f32[9,2048]{0,1:T(8,128)S(1)} fusion(s32[1024]{0:T(1024)S(1)} %get-tuple-element.215, f32[1024,9]{1,0:T(8,128)S(1)} %copy.62, f32[]{:T(128)} %constant.193.clone.1), kind=kCustom, calls=%fused_computation.138 | custom fusion | bytes 73732 | tf_op jit(solution)/shard_map/scatter | solution.py:210
  204.7 23.1 %all_to_all.19 = f32[128,1,144]{2,1,0:T(1,128)S(1)} all-to-all(f32[128,1,144]{2,1,0:T(1,128)S(1)} %reshape.323), channel_id=1, replica_groups=mesh['view'=4,'dev'=128] {'dev'}, dimensions={0} | all-to-all | bytes 147456 | tf_op jit(solution)/shard_map/all_to_all | solution.py:212
  227.8 0.9 reduce.6
  229.3 11.5 %scatter_custom_fusion.3 = f32[9,512]{0,1:T(8,128)S(1)} fusion(s32[2048]{0:T(1024)S(1)} %bitcast.199, f32[2048,9]{1,0:T(8,128)S(1)} %bitcast.148, f32[]{:T(128)} %constant.193.clone.1), kind=kCustom, calls=%fused_computation.144 | custom fusion | flops 18432 | bytes 18436 | tf_op jit(solution)/shard_map/scatter-add | solution.py:219
  243.4 5.7 %fusion.98 = (f32[1,512]{1,0:T(1,128)S(1)}, f32[1,512]{1,0:T(1,128)S(1)}, f32[1,512]{1,0:T(1,128)S(1)}, f32[1,512]{1,0:T(1,128)S(1)}, f32[1,512]{1,0:T(1,128)S(1...) fusion(f32[1,512]{1,0:T(1,128)S(1)} %copy.82, f32[1,512]{1,0:T(1,128)S(1)} %copy.81, ...), kind=kLoop, calls=%fused_computation.325 | loop fusion | flops 81920 | bytes 100388 | tf_op jit(solution)/shard_map/transpose(jvp())/neg | solution.py:87
  249.1 1.9 negate_add_fusion.1
  251.4 2.7 %collective-permute-start = (f32[59,512]{1,0:T(8,128)S(1)}, f32[59,512]{1,0:T(8,128)S(1)}, u32[]{:S(2)}, u32[]{:S(2)}) collective-permute-start(f32[59,512]{1,0:T(8,128)S(1)} %pad_add_fusion.9), channel_id=1, source_target_pairs={{0,128},{128,0},{256,384},{384,256},{1,129},{129,1},{257,385},{385... | collective-permute-start | bytes 362504 | tf_op jit(solution)/shard_map/ppermute | solution.py:223
  254.1 5.3 %collective-permute-done = f32[59,512]{1,0:T(8,128)S(1)} collective-permute-done((f32[59,512]{1,0:T(8,128)S(1)}, f32[59,512]{1,0:T(8,128)S(1)}, u32[]{:S(2)}, u32[]{:S(2)}) %collective-permute-start) | collective-permute-done | bytes 120864 | tf_op jit(solution)/shard_map/ppermute | solution.py:223
  259.4 3.3 %collective-permute-start.1 = (f32[59,512]{1,0:T(8,128)S(1)}, f32[59,512]{1,0:T(8,128)S(1)}, u32[]{:S(2)}, u32[]{:S(2)}) collective-permute-start(f32[59,512]{1,0:T(8,128)S(1)} %add.2205), channel_id=1, source_target_pairs={{0,256},{128,384},{256,0},{384,128},{1,257},{129,385},{257,1},{385... | collective-permute-start | bytes 362504 | tf_op jit(solution)/shard_map/ppermute | solution.py:223
  262.7 5.4 %collective-permute-done.1 = f32[59,512]{1,0:T(8,128)S(1)} collective-permute-done((f32[59,512]{1,0:T(8,128)S(1)}, f32[59,512]{1,0:T(8,128)S(1)}, u32[]{:S(2)}, u32[]{:S(2)}) %collective-permute-start.1) | collective-permute-done | bytes 120864 | tf_op jit(solution)/shard_map/ppermute | solution.py:223
  (883 shorter events, 84.2 us)
Async XLA Ops:
  11.9 28.6 %copy-start.11 = (f32[59,512]{1,0:T(8,128)S(1)}, f32[59,512]{1,0:T(8,128)}, u32[]{:S(2)}) copy-start(f32[59,512]{1,0:T(8,128)} %param.8) | copy-start | bytes 362500
  21.3 48.5 %all-to-all-start = ((s32[128,1,16]{2,1,0:T(1,128)}), s32[128,1,16]{2,1,0:T(1,128)S(1)}, u32[]{:S(2)}, u32[]{:S(2)}) async-start(s32[128,1,16]{2,1,0:T(1,128)} %bitcast.48), calls=%async_computation | async-start | bytes 131072 | tf_op jit(solution)/shard_map/all_to_all | solution.py:194
  78.2 16.3 %copy-start.15 = (f32[1,3,4,256]{3,2,1,0:T(4,128)S(1)}, f32[1,3,4,256]{3,2,1,0:T(4,128)}, u32[]{:S(2)}) copy-start(f32[1,3,4,256]{3,2,1,0:T(4,128)} %param.13) | copy-start | bytes 36868
  78.2 33.4 %all-to-all-start.1 = ((f32[128,1,144]{2,1,0:T(1,128)}), f32[128,1,144]{2,1,0:T(1,128)S(1)}, u32[]{:S(2)}, u32[]{:S(2)}) async-start(f32[128,1,144]{2,1,0:T(1,128)} %reshape.321), calls=%async_computation.1 | async-start | bytes 262144 | tf_op jit(solution)/shard_map/all_to_all | solution.py:204
  122.2 11.1 %copy-start = (f32[256,128]{0,1:T(8,128)}, f32[256,128]{0,1:T(8,128)S(1)}, u32[]{:S(2)}) copy-start(f32[256,128]{0,1:T(8,128)S(1)} %slice.1658) | copy-start | bytes 393220 | tf_op jit(solution)/shard_map/while
  126.3 5.5 %copy-start.2 = (f32[256,64]{0,1:T(8,128)}, f32[256,64]{0,1:T(8,128)S(1)}, u32[]{:S(2)}) copy-start(f32[256,64]{0,1:T(8,128)S(1)} %slice.1665) | copy-start | bytes 196612 | tf_op jit(solution)/shard_map/while
  126.4 3.9 %copy-start.4 = (f32[256,32]{0,1:T(8,128)}, f32[256,32]{0,1:T(8,128)S(1)}, u32[]{:S(2)}) copy-start(f32[256,32]{0,1:T(8,128)S(1)} %slice.1666) | copy-start | bytes 98308 | tf_op jit(solution)/shard_map/while
  126.5 2.4 copy-start.6
  126.6 1.6 copy-start.8
  142.8 11.1 %copy-start = (f32[256,128]{0,1:T(8,128)}, f32[256,128]{0,1:T(8,128)S(1)}, u32[]{:S(2)}) copy-start(f32[256,128]{0,1:T(8,128)S(1)} %slice.1658) | copy-start | bytes 393220 | tf_op jit(solution)/shard_map/while
  146.9 5.5 %copy-start.2 = (f32[256,64]{0,1:T(8,128)}, f32[256,64]{0,1:T(8,128)S(1)}, u32[]{:S(2)}) copy-start(f32[256,64]{0,1:T(8,128)S(1)} %slice.1665) | copy-start | bytes 196612 | tf_op jit(solution)/shard_map/while
  147.0 3.9 %copy-start.4 = (f32[256,32]{0,1:T(8,128)}, f32[256,32]{0,1:T(8,128)S(1)}, u32[]{:S(2)}) copy-start(f32[256,32]{0,1:T(8,128)S(1)} %slice.1666) | copy-start | bytes 98308 | tf_op jit(solution)/shard_map/while
  147.1 2.4 copy-start.6
  147.2 1.6 copy-start.8
  163.4 11.1 %copy-start = (f32[256,128]{0,1:T(8,128)}, f32[256,128]{0,1:T(8,128)S(1)}, u32[]{:S(2)}) copy-start(f32[256,128]{0,1:T(8,128)S(1)} %slice.1658) | copy-start | bytes 393220 | tf_op jit(solution)/shard_map/while
  167.5 5.5 %copy-start.2 = (f32[256,64]{0,1:T(8,128)}, f32[256,64]{0,1:T(8,128)S(1)}, u32[]{:S(2)}) copy-start(f32[256,64]{0,1:T(8,128)S(1)} %slice.1665) | copy-start | bytes 196612 | tf_op jit(solution)/shard_map/while
  167.6 3.9 %copy-start.4 = (f32[256,32]{0,1:T(8,128)}, f32[256,32]{0,1:T(8,128)S(1)}, u32[]{:S(2)}) copy-start(f32[256,32]{0,1:T(8,128)S(1)} %slice.1666) | copy-start | bytes 98308 | tf_op jit(solution)/shard_map/while
  167.7 2.4 copy-start.6
  184.0 11.1 %copy-start = (f32[256,128]{0,1:T(8,128)}, f32[256,128]{0,1:T(8,128)S(1)}, u32[]{:S(2)}) copy-start(f32[256,128]{0,1:T(8,128)S(1)} %slice.1658) | copy-start | bytes 393220 | tf_op jit(solution)/shard_map/while
  188.1 5.5 %copy-start.2 = (f32[256,64]{0,1:T(8,128)}, f32[256,64]{0,1:T(8,128)S(1)}, u32[]{:S(2)}) copy-start(f32[256,64]{0,1:T(8,128)S(1)} %slice.1665) | copy-start | bytes 196612 | tf_op jit(solution)/shard_map/while
  188.2 3.9 %copy-start.4 = (f32[256,32]{0,1:T(8,128)}, f32[256,32]{0,1:T(8,128)S(1)}, u32[]{:S(2)}) copy-start(f32[256,32]{0,1:T(8,128)S(1)} %slice.1666) | copy-start | bytes 98308 | tf_op jit(solution)/shard_map/while
  188.3 2.4 copy-start.6
  251.4 8.0 %collective-permute-start = (f32[59,512]{1,0:T(8,128)S(1)}, f32[59,512]{1,0:T(8,128)S(1)}, u32[]{:S(2)}, u32[]{:S(2)}) collective-permute-start(f32[59,512]{1,0:T(8,128)S(1)} %pad_add_fusion.9), channel_id=1, source_target_pairs={{0,128},{128,0},{256,384},{384,256},{1,129},{129,1},{257,385},{385... | collective-permute-start | bytes 362504 | tf_op jit(solution)/shard_map/ppermute | solution.py:223
  259.4 8.7 %collective-permute-start.1 = (f32[59,512]{1,0:T(8,128)S(1)}, f32[59,512]{1,0:T(8,128)S(1)}, u32[]{:S(2)}, u32[]{:S(2)}) collective-permute-start(f32[59,512]{1,0:T(8,128)S(1)} %add.2205), channel_id=1, source_target_pairs={{0,256},{128,384},{256,0},{384,128},{1,257},{129,385},{257,1},{385... | collective-permute-start | bytes 362504 | tf_op jit(solution)/shard_map/ppermute | solution.py:223
  (78 other events, 52.8 us)
